TPU v7x, 512 devices: a whole 4x8x8 slice. The times are simulated.
512 devices in a mesh: dp: 16 (over z_hi, y), ctx: 32 (over x, z_lo, core).
Axes of the slice: x: 4, y: 8, z: 8 (z_hi: 2, z_lo: 4; z = z_hi * 4 + z_lo), core: 2. Of those that a mesh axis runs over, the one named last changes fastest.
Arguments:
- queries: bfloat16 [65536, 4096], P(('dp', 'ctx')), may hold values from -6 to 6
- keys: bfloat16 [65536, 512], P(('dp', 'ctx')), may hold values from -6 to 6
- values: bfloat16 [65536, 512], P(('dp', 'ctx')), may hold values from -6 to 6
- out_grad: bfloat16 [65536, 4096], P(('dp', 'ctx')), may hold values from -6 to 6
- inputs: bfloat16 [65536, 5120], P(('dp', 'ctx')), may hold values from -24 to 24
- permutation: int32 [16, 64], P('dp'), may hold values from 0 to 63, each once within a row
- lengths: int32 [16, 4], P('dp'), may hold values from 1 to 2048, 4096 in all within a row
Outputs:
- query_grad: bfloat16 [65536, 4096], P(('dp', 'ctx'))
- kv_grad: bfloat16 [65536, 1024], P(('dp', 'ctx'))
- weight_grad: float32 [5120, 1024], P(('dp', 'ctx'))
Inputs may be any that keep to these rules, and one draw needn't show every extreme that they name: `lengths`: each row sums to 4096; its largest entry is 2048.
All inputs are finite; a program needn't handle non-finite values.
Results may differ from a plain program's by a relative error of at most 0.011.
Values may be sent and summed in bfloat16 or wider, within the bound.
A program may use at most 64 MiB of HBM per device.

v0:
```python
import jax
import jax.numpy as jnp
from jax import lax
from jax.sharding import PartitionSpec as P

DH = 128


def from_behind(value, axis, by):
    size = lax.axis_size(axis)
    return lax.ppermute(value, axis, [(i, (i + by) % size) for i in range(size)])


def attention_grads(
    queries, key_rows, value_rows, out_grad, query_pos, key_pos, query_seg, key_seg
):
    rows = queries.shape[0]
    width = key_rows.shape[0]
    groups = key_rows.shape[1] // DH
    shared = queries.shape[1] // (DH * groups)
    scale = 1.0 / DH**0.5
    query_view = queries.reshape(rows, groups, shared, DH)
    key_view = key_rows.reshape(width, groups, DH)
    value_view = value_rows.reshape(width, groups, DH)
    grad_view = out_grad.reshape(rows, groups, shared, DH)
    allowed = (key_pos[None, :] <= query_pos[:, None]) & (key_seg[None, :] == query_seg[:, None])
    score = (
        jnp.einsum("rgqd,kgd->gqrk", query_view, key_view, preferred_element_type=jnp.float32)
        * scale
    )
    masked = jnp.where(allowed, score, -1e30)
    top = jnp.max(masked, axis=-1, keepdims=True)
    expo = jnp.where(allowed, jnp.exp(masked - top), 0.0)
    prob = expo / jnp.sum(expo, axis=-1, keepdims=True)
    prob_low = prob.astype(jnp.bfloat16)
    output = jnp.einsum("gqrk,kgd->rgqd", prob_low, value_view, preferred_element_type=jnp.float32)
    delta = jnp.sum(grad_view.astype(jnp.float32) * output, axis=-1)
    dprob = jnp.einsum("rgqd,kgd->gqrk", grad_view, value_view, preferred_element_type=jnp.float32)
    dscore = (prob * (dprob - jnp.transpose(delta, (1, 2, 0))[..., None])).astype(jnp.bfloat16)
    query_grad = (
        jnp.einsum("gqrk,kgd->rgqd", dscore, key_view, preferred_element_type=jnp.float32) * scale
    )
    key_part = (
        jnp.einsum("gqrk,rgqd->kgd", dscore, query_view, preferred_element_type=jnp.float32) * scale
    )
    value_part = jnp.einsum(
        "gqrk,rgqd->kgd", prob_low, grad_view, preferred_element_type=jnp.float32
    )
    return (
        query_grad.astype(jnp.bfloat16).reshape(rows, queries.shape[1]),
        key_part.reshape(width, groups * DH),
        value_part.reshape(width, groups * DH),
    )


def folder(features, piece):
    return jnp.einsum("dt,tc->dc", features, piece, preferred_element_type=jnp.float32)


def body(queries, keys, values, out_grad, inputs, permutation, lengths):
    rows = queries.shape[0]
    span = rows // 2
    cycle = lax.axis_size("ctx")
    place = lax.axis_index("ctx")
    order = permutation[0]
    own_slots = lax.dynamic_slice(order, (2 * place,), (2,))
    prior_slots = lax.dynamic_slice(order, (2 * ((place + cycle - 1) % cycle),), (2,))
    offsets = jnp.arange(span, dtype=jnp.int32)
    query_pos = (own_slots[:, None] * span + offsets[None, :]).reshape(rows)
    prior_pos = (prior_slots[:, None] * span + offsets[None, :]).reshape(rows)
    key_pos = jnp.concatenate([prior_pos, query_pos], axis=0)
    bounds = jnp.cumsum(lengths[0])[:-1]
    query_seg = jnp.sum((query_pos[:, None] >= bounds[None, :]).astype(jnp.int32), axis=1)
    key_seg = jnp.sum((key_pos[:, None] >= bounds[None, :]).astype(jnp.int32), axis=1)
    prior_keys, prior_values = from_behind((keys, values), "ctx", 1)
    key_rows = jnp.concatenate([prior_keys, keys], axis=0)
    value_rows = jnp.concatenate([prior_values, values], axis=0)
    query_grad, key_part, value_part = attention_grads(
        queries, key_rows, value_rows, out_grad, query_pos, key_pos, query_seg, key_seg
    )
    back_keys, back_values = from_behind((key_part[:rows], value_part[:rows]), "ctx", -1)
    kv_grad = jnp.concatenate(
        [key_part[rows:] + back_keys, value_part[rows:] + back_values], axis=1
    )
    kv_grad = kv_grad.astype(jnp.bfloat16)
    groups = lax.axis_size("dp")
    model_width = inputs.shape[1]
    piece_width = model_width // (groups * cycle)
    columns = kv_grad.shape[1]
    turned = jnp.transpose(inputs)
    spread = turned.reshape(groups, cycle, piece_width, rows)
    features = lax.all_to_all(spread, "ctx", split_axis=1, concat_axis=3, tiled=True).reshape(
        groups * piece_width, cycle * rows
    )
    term = folder(features, lax.all_gather(kv_grad, "ctx", axis=0, tiled=True))
    share = lax.psum_scatter(
        term.reshape(groups, piece_width, columns), "dp", scatter_dimension=0, tiled=True
    )
    return (query_grad, kv_grad, share.reshape(piece_width, columns))


def solution(mesh):
    placed = (
        P(("dp", "ctx"), None),
        P(("dp", "ctx"), None),
        P(("dp", "ctx"), None),
        P(("dp", "ctx"), None),
        P(("dp", "ctx"), None),
        P("dp", None),
        P("dp", None),
    )
    return jax.shard_map(
        body,
        mesh=mesh,
        in_specs=placed,
        out_specs=(P(("dp", "ctx"), None), P(("dp", "ctx"), None), P(("dp", "ctx"), None)),
        check_vma=False,
    )
```

profile of v0, /device:TPU:1, one launch (start us, length us, event | category | flops | bytes accessed | tf_op | source)
XLA Modules:
  0.0 377.8 jit_solution(4794067335015709457)
XLA Ops:
  7.2 0.0 copy-start.3
  7.2 0.0 all-gather.2.cloned.1.call-start
  7.2 1.1 copy.72
  8.3 5.4 %collective-permute-start.1 = (bf16[128,512]{0,1:T(8,128)(2,1)S(1)}, bf16[128,512]{0,1:T(8,128)(2,1)S(1)}, u32[]{:S(2)}, u32[]{:S(2)}) collective-permute-start(bf16[128,512]{0,1:T(8,128)(2,1)S(1)} %copy.72), channel_id=1, source_target_pairs={{0,1},{1,2},{2,3},{3,4},{4,5},{5,6},{6,7},{7,8},{8,9},{9,10},{10,1... | collective-permute-start | bytes 393224 | tf_op jit(solution)/shard_map/ppermute | solution.py:11
  13.7 1.0 copy.68
  14.8 1.9 collective-permute-start
  16.7 0.8 reduce-window.4
  17.5 0.8 multiply_bitcast_fusion.1
  18.3 0.1 iota_add_fusion
  18.4 0.1 add.70
  18.5 0.1 add.65
  18.6 0.1 convert_reduce_fusion.1
  18.7 0.1 convert_reduce_fusion
  18.8 1.6 copy.105
  20.4 0.0 copy-done.3
  20.4 0.0 copy-start
  20.4 0.7 copy.74
  21.1 0.1 compare_and_fusion
  21.2 0.0 collective-permute-done
  21.3 0.9 pad_maximum_fusion
  22.2 0.0 copy-start.4
  22.2 3.6 fusion.23
  25.8 0.0 copy-done
  25.8 0.0 copy-done.4
  25.8 2.7 fusion.8
  28.5 0.0 copy-start.2
  28.5 0.8 convolution_bitcast_fusion
  29.3 0.0 collective-permute-done.1
  29.4 0.5 fusion.4
  29.9 0.8 copy-done.2
  30.7 0.0 copy-start.1
  30.7 0.9 fusion.2
  31.6 0.3 copy-done.1
  31.9 0.8 fusion.16
  32.8 0.8 copy.84
  33.6 9.1 %collective-permute-start.3 = (f32[128,512]{1,0:T(8,128)}, f32[128,512]{1,0:T(8,128)}, u32[]{:S(2)}, u32[]{:S(2)}) collective-permute-start(f32[128,512]{1,0:T(8,128)} %copy.84), channel_id=1, source_target_pairs={{0,31},{1,0},{2,1},{3,2},{4,3},{5,4},{6,5},{7,6},{8,7},{9,8},{10,9... | collective-permute-start | bytes 786440 | tf_op jit(solution)/shard_map/ppermute | solution.py:11
  42.8 0.1 copy.81
  42.9 3.8 collective-permute-start.2
  46.7 0.1 copy.82
  46.8 0.1 copy.85
  47.0 0.0 collective-permute-done.3
  47.0 1.0 add_convert_fusion
  48.0 2.7 collective-permute-done.2
  50.7 0.7 pad_maximum_fusion.2
  51.4 0.0 all-gather.2.cloned.1.call-update
  51.4 0.0 reduce-scatter.2.cloned.1.call-start
  51.5 1.8 copy.86
  53.2 1.6 reshape.104
  54.9 3.1 copy.87
  58.0 54.2 %all_to_all.15 = bf16[16,32,10,128]{3,0,2,1:T(8,128)(2,1)S(1)} all-to-all(bf16[16,32,10,128]{3,0,2,1:T(8,128)(2,1)S(1)} %copy.87), channel_id=1, replica_groups=mesh['dp'=16,'ctx'=32] {'ctx'}, dimensions={1} | all-to-all | bytes 2621440 | tf_op jit(solution)/shard_map/all_to_all | solution.py:92
  112.2 0.5 copy.88
  112.7 34.1 %all-gather.2.cloned.1.call-done = bf16[4096,1024]{1,0:T(8,128)(2,1)} async-done(((bf16[128,1024]{1,0:T(8,128)(2,1)}), bf16[4096,1024]{1,0:T(8,128)(2,1)}) %all-gather.2.cloned.1.call-update) | async-done | bytes 8388624 | tf_op jit(solution)/shard_map/all_gather | solution.py:95
  146.8 6.0 %fusion.12 = f32[160,1024]{1,0:T(8,128)} fusion(bf16[4096,1024]{1,0:T(8,128)(2,1)} %all-gather.2.cloned.1.call-done, bf16[20,8,32,128]{3,2,1,0:T(8,128)(2,1)S(1)} %bitcast.106), kind=kOutput, calls=%fused_computation.18 | convolution fusion | flops 1342177280 | bytes 10354688 | tf_op jit(solution)/shard_map/dt,tc->dc/dot_general | solution.py:57
  152.8 0.0 copy-start.5
  152.8 2.2 reshape.106
  155.0 0.0 reduce-scatter.2.cloned.1.call-update
  155.0 0.0 copy-done.5
  155.0 0.5 multiply_convert_fusion
  155.5 1.3 copy.89
  156.8 214.1 %reduce-scatter.2.cloned.1.call-done = f32[1,10,1024]{2,1,0:T(8,128)} async-done(((f32[16,10,1024]{2,1,0:T(8,128)}), f32[1,10,1024]{2,1,0:T(8,128)}) %reduce-scatter.2.cloned.1.call-update) | async-done | bytes 40976 | tf_op jit(solution)/shard_map/reduce_scatter | solution.py:96
  (8 shorter events, 0.2 us)
Async XLA Ops:
  7.2 13.2 %copy-start.3 = (bf16[128,4096]{1,0:T(8,128)(2,1)S(1)}, bf16[128,4096]{1,0:T(8,128)(2,1)}, u32[]{:S(2)}) copy-start(bf16[128,4096]{1,0:T(8,128)(2,1)} %param.10) | copy-start | bytes 3145732
  7.2 139.6 %all-gather.2.cloned.1.call-start = ((), (), s32[]{:S(2)}) async-start(), calls=%async_computation.2 | async-start | bytes 8650752 | tf_op jit(solution)/shard_map/all_gather | solution.py:95
  8.3 21.0 %collective-permute-start.1 = (bf16[128,512]{0,1:T(8,128)(2,1)S(1)}, bf16[128,512]{0,1:T(8,128)(2,1)S(1)}, u32[]{:S(2)}, u32[]{:S(2)}) collective-permute-start(bf16[128,512]{0,1:T(8,128)(2,1)S(1)} %copy.72), channel_id=1, source_target_pairs={{0,1},{1,2},{2,3},{3,4},{4,5},{5,6},{6,7},{7,8},{8,9},{9,10},{10,1... | collective-permute-start | bytes 393224 | tf_op jit(solution)/shard_map/ppermute | solution.py:11
  14.8 6.5 %collective-permute-start = (bf16[128,512]{0,1:T(8,128)(2,1)S(1)}, bf16[128,512]{0,1:T(8,128)(2,1)}, u32[]{:S(2)}, u32[]{:S(2)}) collective-permute-start(bf16[128,512]{0,1:T(8,128)(2,1)S(1)} %copy.68), channel_id=1, source_target_pairs={{0,1},{1,2},{2,3},{3,4},{4,5},{5,6},{6,7},{7,8},{8,9},{9,10},{10,1... | collective-permute-start | bytes 393224 | tf_op jit(solution)/shard_map/ppermute | solution.py:11
  20.4 5.4 %copy-start = (bf16[128,4096]{0,1:T(8,128)(2,1)}, bf16[128,4096]{0,1:T(8,128)(2,1)S(1)}, u32[]{:S(2)}) copy-start(bf16[128,4096]{0,1:T(8,128)(2,1)S(1)} %copy.105) | copy-start | bytes 3145732
  22.2 3.6 copy-start.4
  28.5 2.2 copy-start.2
  30.7 1.2 copy-start.1
  33.6 13.3 %collective-permute-start.3 = (f32[128,512]{1,0:T(8,128)}, f32[128,512]{1,0:T(8,128)}, u32[]{:S(2)}, u32[]{:S(2)}) collective-permute-start(f32[128,512]{1,0:T(8,128)} %copy.84), channel_id=1, source_target_pairs={{0,31},{1,0},{2,1},{3,2},{4,3},{5,4},{6,5},{7,6},{8,7},{9,8},{10,9... | collective-permute-start | bytes 786440 | tf_op jit(solution)/shard_map/ppermute | solution.py:11
  42.9 7.7 %collective-permute-start.2 = (f32[128,512]{1,0:T(8,128)S(1)}, f32[128,512]{1,0:T(8,128)S(1)}, u32[]{:S(2)}, u32[]{:S(2)}) collective-permute-start(f32[128,512]{1,0:T(8,128)S(1)} %copy.81), channel_id=1, source_target_pairs={{0,31},{1,0},{2,1},{3,2},{4,3},{5,4},{6,5},{7,6},{8,7},{9,8},{10,9... | collective-permute-start | bytes 786440 | tf_op jit(solution)/shard_map/ppermute | solution.py:11
  51.4 319.5 %reduce-scatter.2.cloned.1.call-start = ((), (), s32[]{:S(2)}) async-start(), calls=%async_computation.3 | async-start | bytes 1114112 | tf_op jit(solution)/shard_map/reduce_scatter | solution.py:96
  152.8 2.2 copy-start.5
Sparse Core Ops, SparseCore 0:
  51.5 95.2 all-gather.1
  155.1 215.7 reduce-scatter.1
where the time goes:
time: 383 us; the launch traced here: 378 us
  waiting for transfers between devices  251 us (66%)
  blocking collectives  54.2 us (14%)
  starting transfers between devices  20.3 us (5%)
  local copies, waits for them, and re-layouts  17.5 us (5%)
  between operations  14.3 us (4%)
  matrix products  13.1 us (3%)
  other arithmetic  7.44 us (2%)
    reduce_scatter x1, waiting for transfers between devices, body(): lax.psum_scatter(term.reshape(groups, piece_width, columns), 'dp', scatte...  214 us
    all_to_all x1, blocking collectives, body(): lax.all_to_all(spread, 'ctx', split_axis=1, concat_axis=3, tiled=True)  54.2 us
    all_gather x1, waiting for transfers between devices, body(): term = folder(features, lax.all_gather(kv_grad, 'ctx', axis=0, tiled=True))  34.1 us
    ppermute x4, starting transfers between devices, from_behind(): lax.ppermute(value, axis, [(i, (i + by) % size) for i in range(size)])  20.2 us
  transfers between devices with their start and end apart: 6, of which 3 were waited for; matrix products, arithmetic and copies ran while one was open for 6% of the time, Pallas kernels for 0%

commit v1 on v0

v1 whole, which is shorter than its diff:
```python
import functools
import math

import jax
import jax.numpy as jnp
from jax import lax
from jax.experimental import pallas as pl
from jax.experimental.pallas import tpu as pltpu
from jax.sharding import PartitionSpec as P

DH = 128
NZH, NY, NX, NZL, NC = 2, 8, 4, 4, 2
NZ = NZH * NZL
PAIR = 2
PAD = 16
MESH = pl.DeviceIdType.MESH
F32, BF16 = jnp.float32, jnp.bfloat16
NT = (((1,), (1,)), ((), ()))
NN = (((1,), (0,)), ((), ()))
TN = (((0,), (0,)), ((), ()))


def dot(a, b, dims):
    return lax.dot_general(a, b, dims, preferred_element_type=F32)


def kernel(
    order, lens, q_hbm, k_hbm, v_hbm, og_hbm, x_hbm, qg_out, kv_out, w_out,
    x_v, q_v, og_v, kall, vall, bias, qg_v, acc, back, brecv, kvg, gbuf, xt, xr,
    ys, yr, pf, zf, zs, zr, ry, rz, s2y, r2y, s2z, r2z,
    loc, kvo_sem, kv_s, kv_r, x_s, x_r, f_s, f_r, b_s, b_r, g_s, g_r,
    ys_s, ys_r, zs_s, zs_r, y2_s, y2_r, z2_s, z2_r,
):
    rows = k_hbm.shape[0]
    span = rows // 2
    heads = k_hbm.shape[1] // DH
    shared = q_hbm.shape[1] // (DH * heads)
    chunks = heads // PAIR
    width = PAIR * DH
    own = w_out.shape[0]
    octet = NZL * NC * own
    scale = 1.0 / DH**0.5

    dp, ctx = lax.axis_index("dp"), lax.axis_index("ctx")
    cycle = NX * NZL * NC
    zhi, y = dp // NY, dp % NY
    x, zlo, core = ctx // (NZL * NC), (ctx // NC) % NZL, ctx % NC
    z = zhi * NZL + zlo
    after, before = (ctx + 1) % cycle, (ctx + cycle - 1) % cycle

    def at_x(d, e):
        return (dp, ((x + d) % NX) * (NZL * NC) + zlo * NC + (core + e) % NC)

    def at_y(d, e):
        return (zhi * NY + (y + d) % NY, x * (NZL * NC) + zlo * NC + (core + e) % NC)

    def at_z(d, e):
        to = (z + d) % NZ
        return ((to // NZL) * NY + y, x * (NZL * NC) + (to % NZL) * NC + (core + e) % NC)

    def remote(src, dst, send, recv, to):
        return pltpu.make_async_remote_copy(
            src_ref=src, dst_ref=dst, send_sem=send, recv_sem=recv, device_id=to, device_id_type=MESH
        )

    load_x = pltpu.make_async_copy(x_hbm, x_v, loc.at[0])
    load_k = pltpu.make_async_copy(k_hbm, kall.at[pl.ds(rows, rows)], loc.at[1])
    load_v = pltpu.make_async_copy(v_hbm, vall.at[pl.ds(rows, rows)], loc.at[2])
    load_q = pltpu.make_async_copy(q_hbm, q_v, loc.at[3])
    load_og = pltpu.make_async_copy(og_hbm, og_v, loc.at[4])
    for load in (load_x, load_k, load_v, load_q, load_og):
        load.start()

    partners = [(dp, after), (dp, before)]
    partners += [at_x(d, e) for d in range(NX) for e in range(NC) if d or e]
    partners += [at_y(d, e) for d in range(1, NY) for e in range(NC)]
    partners += [at_z(d, e) for d in range(1, NZ) for e in range(NC)]
    barrier = pltpu.get_barrier_semaphore()
    for to in partners:
        pl.semaphore_signal(barrier, inc=1, device_id=to, device_id_type=MESH)
    pl.semaphore_wait(barrier, len(partners))

    kv_copies = [
        remote(k_hbm, kall.at[pl.ds(0, rows)], kv_s.at[0], kv_r.at[0], (dp, after)),
        remote(v_hbm, vall.at[pl.ds(0, rows)], kv_s.at[1], kv_r.at[1], (dp, after)),
    ]
    for copy in kv_copies:
        copy.start()

    load_x.wait()
    two = 2 * NX * octet
    for i in range(NZH * NY // 2):
        turned = jnp.transpose(x_v[:, i * two : (i + 1) * two])
        xt[2 * i : 2 * i + 2] = turned.reshape(2, NX, octet, rows)
    x_copies = []
    for d in (2, 1, 3) if NX == 4 else range(1, NX):
        copy = remote(
            xt.at[:, (x + d) % NX], xr.at[:, :, pl.ds(d * rows, rows)],
            x_s.at[d], x_r.at[d], at_x(d, 0),
        )
        copy.start()
        x_copies.append(copy)
    own_x = pltpu.make_async_copy(xt.at[:, x], xr.at[:, :, pl.ds(0, rows)], loc.at[5])
    own_x.start()

    prior = (ctx + cycle - 1) % cycle
    key_slots = [order[0, 2 * prior], order[0, 2 * prior + 1], order[0, 2 * ctx], order[0, 2 * ctx + 1]]
    bounds = [lens[0, 0]]
    for i in range(1, lens.shape[1] - 1):
        bounds.append(bounds[-1] + lens[0, i])

    def rank(pos):
        seg = jnp.zeros(pos.shape, jnp.int32)
        for bound in bounds:
            seg = seg + (pos >= bound).astype(jnp.int32)
        return seg

    shape = (2 * rows, rows)
    key_at = lax.broadcasted_iota(jnp.int32, shape, 0)
    query_at = lax.broadcasted_iota(jnp.int32, shape, 1)
    key_slot = jnp.where(
        key_at < rows,
        jnp.where(key_at < span, key_slots[0], key_slots[1]),
        jnp.where(key_at < rows + span, key_slots[2], key_slots[3]),
    )
    query_slot = jnp.where(query_at < span, key_slots[2], key_slots[3])
    key_pos = key_slot * span + key_at % span
    query_pos = query_slot * span + query_at % span
    allowed = (key_pos <= query_pos) & (rank(key_pos) == rank(query_pos))
    term = jnp.where(allowed, 0.0, -1e30).astype(F32)
    bias[:, :rows] = term
    bias[:, rows:] = term

    own_x.wait()
    hand_own = remote(
        xr.at[:, :, pl.ds(0, rows)], xr.at[:, :, pl.ds(NX * rows, rows)], f_s.at[0], f_r.at[0], at_x(0, 1)
    )
    hand_own.start()
    hands = [hand_own]

    load_k.wait()
    load_v.wait()
    load_q.wait()
    load_og.wait()
    for copy in kv_copies:
        copy.wait_recv()

    def attend(c):
        def one_head(i, carry):
            head = c * PAIR + i
            lanes = pl.ds(pl.multiple_of(head * DH, DH), DH)
            keys, values = kall[:, lanes], vall[:, lanes]
            key_sum = value_sum = None
            for p in range(shared // 2):
                first = (head * shared + 2 * p) * DH
                cols = [pl.ds(pl.multiple_of(first + j * DH, DH), DH) for j in range(2)]
                query = jnp.concatenate([q_v[:, cols[0]], q_v[:, cols[1]]], axis=0)
                grad = jnp.concatenate([og_v[:, cols[0]], og_v[:, cols[1]]], axis=0)
                score = dot(keys, query, NT) + bias[...]
                top = jnp.max(score, axis=0, keepdims=True)
                expo = jnp.exp2((score - top) * (scale * math.log2(math.e)))
                prob = expo * (1.0 / jnp.sum(expo, axis=0, keepdims=True))
                prob_low = prob.astype(BF16)
                dprob = dot(values, grad, NT)
                delta = jnp.sum(prob_low.astype(F32) * dprob, axis=0, keepdims=True)
                dscore = (prob * (dprob - delta)).astype(BF16)
                query_grad = (dot(dscore, keys, TN) * scale).astype(BF16)
                qg_v[:, cols[0]] = query_grad[:rows]
                qg_v[:, cols[1]] = query_grad[rows:]
                key_term = dot(dscore, query, NN)
                value_term = dot(prob_low, grad, NN)
                key_sum = key_term if p == 0 else key_sum + key_term
                value_sum = value_term if p == 0 else value_sum + value_term
            key_sum = key_sum * scale
            spot = pl.ds(pl.multiple_of(i * DH, DH), DH)
            acc[c, 0, :, spot] = key_sum[rows:]
            acc[c, 1, :, spot] = value_sum[rows:]
            back[c, 0, :, spot] = key_sum[:rows].astype(BF16)
            back[c, 1, :, spot] = value_sum[:rows].astype(BF16)
            return carry

        lax.fori_loop(0, PAIR, one_head, 0)

    back_copies, out_copies = [], []
    for c in range(chunks):
        attend(c)
        copy = remote(back.at[c], brecv.at[c], b_s.at[c], b_r.at[c], (dp, before))
        copy.start()
        back_copies.append(copy)
        wide = PAIR * shared * DH
        cols = pl.ds(c * wide, wide)
        copy = pltpu.make_async_copy(qg_v.at[:, cols], qg_out.at[:, cols], kvo_sem.at[c])
        copy.start()
        out_copies.append(copy)

    g_copies = []

    def finish(c):
        back_copies[c].wait_recv()
        for t in range(2):
            kvg[c, t] = (acc[c, t] + brecv[c, t].astype(F32)).astype(BF16)
        gbuf[c, 0] = kvg[c, core]
        copies = []
        for d in (2, 1, 3, 0) if NX == 4 else range(NX):
            for e in range(NC):
                if d or e:
                    slot = e * NX + d
                    copy = remote(
                        kvg.at[c, (core + e) % NC], gbuf.at[c, slot],
                        g_s.at[c, slot], g_r.at[c, slot], at_x(d, e),
                    )
                    copy.start()
                    copies.append(copy)
        g_copies.append(copies)
        for t in range(2):
            cols = pl.ds(t * heads * DH + c * width, width)
            copy = pltpu.make_async_copy(kvg.at[c, t], kv_out.at[:, cols], kvo_sem.at[chunks + 2 * c + t])
            copy.start()
            out_copies.append(copy)

    finish(0)

    for copy, d in zip(x_copies, (2, 1, 3) if NX == 4 else range(1, NX)):
        copy.wait_recv()
        hand = remote(
            xr.at[:, :, pl.ds(d * rows, rows)], xr.at[:, :, pl.ds((NX + d) * rows, rows)],
            f_s.at[d], f_r.at[d], at_x(0, 1),
        )
        hand.start()
        hands.append(hand)

    for c in range(1, chunks):
        finish(c)
    for hand in hands:
        hand.wait_recv()

    far_y = sorted(range(1, NY), key=lambda d: -min(d, NY - d))
    far_z = sorted(range(1, NZ), key=lambda d: -min(d, NZ - d))
    y_copies, z_copies = [], []
    piece = NC * own

    def multiply(c):
        for copy in g_copies[c]:
            copy.wait_recv()
        right = gbuf[c].reshape(NX * NC * rows, width)
        for h in range(NZH):
            left = xr[h * NY : (h + 1) * NY].reshape(NY * octet, NX * NC * rows)
            part = dot(left, right, NN)
            ys[c, h] = part[:, :DH].astype(BF16).reshape(NY, octet, DH)
            pf[...] = part[:, DH:]
            for i in range(NY):
                for j in range(NZL):
                    zf[h * NZL + j, i * piece : (i + 1) * piece] = pf[
                        i * octet + j * piece : i * octet + (j + 1) * piece
                    ]
        zs[c] = zf[...].astype(BF16)
        copies = []
        for d in far_y:
            copy = remote(
                ys.at[c, :, (y + d) % NY], yr.at[c, d - 1], ys_s.at[c, d - 1], ys_r.at[c, d - 1], at_y(d, 0)
            )
            copy.start()
            copies.append(copy)
        y_copies.append(copies)
        copies = []
        for d in far_z:
            copy = remote(
                zs.at[c, (z + d) % NZ], zr.at[c, d - 1], zs_s.at[c, d - 1], zs_r.at[c, d - 1], at_z(d, 0)
            )
            copy.start()
            copies.append(copy)
        z_copies.append(copies)

    for c in range(chunks):
        multiply(c)

    ends = []

    def second(send_from, land, send, recv, where, spot, count):
        for d in range(count):
            for e in range(NC):
                if d or e:
                    copy = remote(
                        send_from.at[spot(d), (core + e) % NC], land.at[d * NC + e], send, recv, where(d, e)
                    )
                    copy.start()
        land[0] = send_from[spot(0), core]
        ends.append((land, send, recv))

    ry[:, octet:] = jnp.zeros((NZH, ry.shape[1] - octet, DH), F32)
    rz[NY * piece :] = jnp.zeros((rz.shape[0] - NY * piece, DH), F32)

    def reduce(c):
        total = ys[c, :, y].astype(F32)
        for copy in y_copies[c]:
            copy.wait_recv()
        for d in range(NY - 1):
            total = total + yr[c, d].astype(F32)
        ry[:, :octet] = total
        for h in range(NZH):
            for j in range(NZL):
                for k in range(NC):
                    start = (j * NC + k) * own
                    s2y[c, h * NZL + j, k] = ry[h, start : start + PAD].astype(BF16)
        second(
            s2y.at[c], r2y.at[c], y2_s.at[c], y2_r.at[c], at_z, lambda d: (z + d) % NZ, NZ
        )
        total = zs[c, z].astype(F32)
        for copy in z_copies[c]:
            copy.wait_recv()
        for d in range(NZ - 1):
            total = total + zr[c, d].astype(F32)
        rz[: NY * piece] = total
        for i in range(NY):
            for k in range(NC):
                start = (i * NC + k) * own
                s2z[c, i, k] = rz[start : start + PAD].astype(BF16)
        second(
            s2z.at[c], r2z.at[c], z2_s.at[c], z2_r.at[c], at_y, lambda d: (y + d) % NY, NY
        )

    for c in range(chunks):
        reduce(c)

    for c in range(chunks):
        for kind in range(2):
            land, send, recv = ends[2 * c + kind]
            others = land.at[pl.ds(1, land.shape[0] - 1)]
            pltpu.make_async_copy(others, others, recv).wait()
            for e in range(NC):
                total = land[e].astype(F32)
                for d in range(1, land.shape[0] // NC):
                    total = total + land[d * NC + e].astype(F32)
                col = ((core + e) % NC) * heads * DH + c * width + kind * DH
                w_out[:, pl.ds(pl.multiple_of(col, DH), DH)] = total[:own]

    for copy in kv_copies + x_copies + hands + back_copies:
        copy.wait_send()
    for copies in g_copies + y_copies + z_copies:
        for copy in copies:
            copy.wait_send()
    for land, send, recv in ends:
        others = land.at[pl.ds(1, land.shape[0] - 1)]
        pltpu.make_async_copy(others, others, send).wait()
    for copy in out_copies:
        copy.wait()


def body(queries, keys, values, out_grad, inputs, permutation, lengths):
    rows, model = inputs.shape
    heads = keys.shape[1] // DH
    chunks = heads // PAIR
    width = PAIR * DH
    own = model // (NZH * NY * NX * NZL * NC)
    octet = NZL * NC * own
    piece = NC * own
    room = lambda n: -(-(n - own + PAD) // 8) * 8
    vmem = lambda shape, kind: pltpu.VMEM(shape, kind)
    dma = lambda *shape: pltpu.SemaphoreType.DMA(shape)
    scratch = [
        vmem((rows, model), BF16),
        vmem(queries.shape, BF16),
        vmem(queries.shape, BF16),
        vmem((2 * rows, heads * DH), BF16),
        vmem((2 * rows, heads * DH), BF16),
        vmem((2 * rows, 2 * rows), F32),
        vmem(queries.shape, BF16),
        vmem((chunks, 2, rows, width), F32),
        vmem((chunks, 2, rows, width), BF16),
        vmem((chunks, 2, rows, width), BF16),
        vmem((chunks, 2, rows, width), BF16),
        vmem((chunks, NX * NC, rows, width), BF16),
        vmem((NZH * NY, NX, octet, rows), BF16),
        vmem((NZH * NY, octet, NX * NC * rows), BF16),
        vmem((chunks, NZH, NY, octet, DH), BF16),
        vmem((chunks, NY - 1, NZH, octet, DH), BF16),
        vmem((NY * octet, DH), F32),
        vmem((NZ, NY * piece, DH), F32),
        vmem((chunks, NZ, NY * piece, DH), BF16),
        vmem((chunks, NZ - 1, NY * piece, DH), BF16),
        vmem((NZH, room(octet), DH), F32),
        vmem((room(NY * piece), DH), F32),
        vmem((chunks, NZ, NC, PAD, DH), BF16),
        vmem((chunks, NZ * NC, PAD, DH), BF16),
        vmem((chunks, NY, NC, PAD, DH), BF16),
        vmem((chunks, NY * NC, PAD, DH), BF16),
        dma(6), dma(3 * chunks),
        dma(2), dma(2),
        dma(NX), dma(NX), dma(NX), dma(NX),
        dma(chunks), dma(chunks),
        dma(chunks, NX * NC), dma(chunks, NX * NC),
        dma(chunks, NY - 1), dma(chunks, NY - 1),
        dma(chunks, NZ - 1), dma(chunks, NZ - 1),
        dma(chunks), dma(chunks), dma(chunks), dma(chunks),
    ]
    smem = pl.BlockSpec(memory_space=pltpu.SMEM)
    anywhere = pl.BlockSpec(memory_space=pl.ANY)
    return pl.pallas_call(
        kernel,
        out_shape=(
            jax.ShapeDtypeStruct(queries.shape, BF16),
            jax.ShapeDtypeStruct((rows, 2 * heads * DH), BF16),
            jax.ShapeDtypeStruct((own, 2 * heads * DH), F32),
        ),
        in_specs=[smem, smem] + [anywhere] * 5,
        out_specs=(anywhere, anywhere, pl.BlockSpec(memory_space=pltpu.VMEM)),
        scratch_shapes=scratch,
        compiler_params=pltpu.CompilerParams(
            collective_id=0, has_side_effects=True, vmem_limit_bytes=48 * 1024 * 1024
        ),
    )(permutation, lengths, queries, keys, values, out_grad, inputs)


def solution(mesh):
    both = P(("dp", "ctx"), None)
    return jax.shard_map(
        body,
        mesh=mesh,
        in_specs=(both, both, both, both, both, P("dp", None), P("dp", None)),
        out_specs=(both, both, both),
        check_vma=False,
    )
```

time: 383 us -> 75.7 us (0.20); the launches traced: 378 us -> 75.4 us
  waiting for transfers between devices: 251 us -> 0 us
  Pallas kernels: 0 us -> 65.6 us
  blocking collectives: 54.2 us -> 0 us
  starting transfers between devices: 20.3 us -> 0 us
  between operations: 14.3 us -> 0.66 us
  matrix products: 13.1 us -> 0 us
  local copies, waits for them, and re-layouts: 17.5 us -> 9.18 us
  other arithmetic: 7.44 us -> 0 us
    reduce_scatter x1 -> x0, waiting for transfers between devices: 214 us -> none  [body(): lax.psum_scatter(term.reshape(groups, piece_width, columns), 'dp', scatte...]
    pallas_call x0 -> x1, Pallas kernels: none -> 65.6 us  [body(): pl.pallas_call(kernel, out_shape=(jax.ShapeDtypeStruct(queries.shape, BF1...]
    all_to_all x1 -> x0, blocking collectives: 54.2 us -> none  [body(): lax.all_to_all(spread, 'ctx', split_axis=1, concat_axis=3, tiled=True)]
    all_gather x1 -> x0, waiting for transfers between devices: 34.1 us -> none  [body(): term = folder(features, lax.all_gather(kv_grad, 'ctx', axis=0, tiled=True))]
    ppermute x4 -> x0, starting transfers between devices: 20.2 us -> none  [from_behind(): lax.ppermute(value, axis, [(i, (i + by) % size) for i in range(size)])]
    dot_general x6 -> x0, matrix products: 9.48 us -> none  [the longest x1 5.99 us: folder(): jnp.einsum('dt,tc->dc', features, piece, preferred_element_type=jnp.float32)]
    reshape x4 -> x0, local copies, waits for them, and re-layouts: 8.55 us -> none  [the longest x2 4.72 us: body(): spread = turned.reshape(groups, cycle, piece_width, rows)]
    unnamed x17, local copies, waits for them, and re-layouts: 5.25 us -> 9.18 us
  transfers between devices with their start and end apart: 6 -> 0, of which waited for: 3 -> 0; matrix products, arithmetic and copies ran while one was open for 6% -> 0% of each run, Pallas kernels for 0% -> 0%
where the time goes in v1:
time: 75.7 us; the launch traced here: 75.4 us
  Pallas kernels  65.6 us (87%)
  local copies, waits for them, and re-layouts  9.18 us (12%)
    pallas_call x1, Pallas kernels, body(): pl.pallas_call(kernel, out_shape=(jax.ShapeDtypeStruct(queries.shape, BF1...  65.6 us
    unnamed x17, local copies, waits for them, and re-layouts  9.18 us

profile of v1, /device:TPU:1, one launch (start us, length us, event | category | flops | bytes accessed | tf_op | source)
XLA Modules:
  0.0 75.4 jit_solution(11299800003179299279)
XLA Ops:
  0.6 0.0 copy-start
  0.6 1.3 %copy-done = bf16[128,5120]{1,0:T(8,128)(2,1)S(1)} copy-done((bf16[128,5120]{1,0:T(8,128)(2,1)S(1)}, bf16[128,5120]{1,0:T(8,128)(2,1)}, u32[]{:S(2)}) %copy-start) | copy-done | bytes 1310744
  1.9 0.0 copy-start.1
  2.0 1.2 %copy-done.1 = bf16[128,4096]{1,0:T(8,128)(2,1)S(1)} copy-done((bf16[128,4096]{1,0:T(8,128)(2,1)S(1)}, bf16[128,4096]{1,0:T(8,128)(2,1)}, u32[]{:S(2)}) %copy-start.1) | copy-done | bytes 1048600
  3.2 0.0 copy-start.2
  3.2 1.2 %copy-done.2 = bf16[128,4096]{1,0:T(8,128)(2,1)S(1)} copy-done((bf16[128,4096]{1,0:T(8,128)(2,1)S(1)}, bf16[128,4096]{1,0:T(8,128)(2,1)}, u32[]{:S(2)}) %copy-start.2) | copy-done | bytes 1048600
  4.4 0.0 copy-start.3
  4.4 0.9 %copy-done.3 = bf16[128,512]{1,0:T(8,128)(2,1)S(1)} copy-done((bf16[128,512]{1,0:T(8,128)(2,1)S(1)}, bf16[128,512]{1,0:T(8,128)(2,1)}, u32[]{:S(2)}) %copy-start.3) | copy-done | bytes 131096
  5.3 0.0 copy-start.4
  5.3 0.9 %copy-done.4 = bf16[128,512]{1,0:T(8,128)(2,1)S(1)} copy-done((bf16[128,512]{1,0:T(8,128)(2,1)S(1)}, bf16[128,512]{1,0:T(8,128)(2,1)}, u32[]{:S(2)}) %copy-start.4) | copy-done | bytes 131096
  6.2 0.0 copy-start.5
  6.2 0.7 copy-done.5
  6.9 0.0 copy-start.6
  6.9 0.7 copy-done.6
  7.5 65.6 %shard_map.94 = (bf16[128,4096]{1,0:T(8,128)(2,1)S(1)}, bf16[128,1024]{1,0:T(8,128)(2,1)S(1)}, f32[10,1024]{1,0:T(8,128)S(1)}) custom-call(s32[1,64]{1,0:T(1,128)S(1)} %copy-done.5, s32[1,4]{1,0:T(1,128)S(1)} %copy-done.6, bf16[128,4096]{1,0:T(8,128)(2,1)S(1)} %copy-done.1, bf16[128,512]{1,0:T(8,128)(2,1)S(1)} %copy-done.3, bf16[128,512]{1,0:T(8,128)(2,1)S(1)} %copy-done.4, ...), custom_call_target="tpu_custom_call" | custom-call | tf_op jit(solution)/shard_map/pallas_call | solution.py:398
  73.1 1.0 %copy.13 = bf16[128,4096]{1,0:T(8,128)(2,1)} copy(bf16[128,4096]{1,0:T(8,128)(2,1)S(1)} %get-tuple-element.6) | data formatting | bytes 2097152
  74.1 0.7 copy.14
  74.8 0.6 copy.15
Async XLA Ops:
  0.6 1.3 %copy-start = (bf16[128,5120]{1,0:T(8,128)(2,1)S(1)}, bf16[128,5120]{1,0:T(8,128)(2,1)}, u32[]{:S(2)}) copy-start(bf16[128,5120]{1,0:T(8,128)(2,1)} %x_hbm.1) | copy-start | bytes 3932164
  1.9 1.2 %copy-start.1 = (bf16[128,4096]{1,0:T(8,128)(2,1)S(1)}, bf16[128,4096]{1,0:T(8,128)(2,1)}, u32[]{:S(2)}) copy-start(bf16[128,4096]{1,0:T(8,128)(2,1)} %q_hbm.1) | copy-start | bytes 3145732
  3.2 1.2 %copy-start.2 = (bf16[128,4096]{1,0:T(8,128)(2,1)S(1)}, bf16[128,4096]{1,0:T(8,128)(2,1)}, u32[]{:S(2)}) copy-start(bf16[128,4096]{1,0:T(8,128)(2,1)} %og_hbm.1) | copy-start | bytes 3145732
  4.4 0.9 %copy-start.3 = (bf16[128,512]{1,0:T(8,128)(2,1)S(1)}, bf16[128,512]{1,0:T(8,128)(2,1)}, u32[]{:S(2)}) copy-start(bf16[128,512]{1,0:T(8,128)(2,1)} %k_hbm.1) | copy-start | bytes 393220
  5.3 0.9 %copy-start.4 = (bf16[128,512]{1,0:T(8,128)(2,1)S(1)}, bf16[128,512]{1,0:T(8,128)(2,1)}, u32[]{:S(2)}) copy-start(bf16[128,512]{1,0:T(8,128)(2,1)} %v_hbm.1) | copy-start | bytes 393220
  6.2 0.7 copy-start.5
  6.9 0.7 copy-start.6

commit v2 on v0

v2 whole, which is shorter than its diff:
```python
import functools
import math

import jax
import jax.numpy as jnp
from jax import lax
from jax.experimental import pallas as pl
from jax.experimental.pallas import tpu as pltpu
from jax.sharding import PartitionSpec as P

DH = 128
NZH, NY, NX, NZL, NC = 2, 8, 4, 4, 2
NZ = NZH * NZL
PAD = 16
FAR = (4, 3, 5, 2, 6, 1, 7)
RELAYED = ()
MESH = pl.DeviceIdType.MESH
F32, BF16 = jnp.float32, jnp.bfloat16
NT = (((1,), (1,)), ((), ()))
NN = (((1,), (0,)), ((), ()))
TN = (((0,), (0,)), ((), ()))


def dot(a, b, dims):
    return lax.dot_general(a, b, dims, preferred_element_type=F32)


def kernel(
    order_hbm, lens_hbm, q_hbm, k_hbm, v_hbm, og_hbm, x_hbm, qg_out, kv_out, w_out,
    order, lens, x_v, qo_v, kv_v, bias, qg_v, acc, back, brecv, kvg, gbuf, xt, xr,
    pf, zf, sent, got, tt, mm, s2, r2, wv,
    loc, out_sem, kv_s, kv_r, x_s, x_r, hand_s, hand_r, b_s, b_r, g_s, g_r, one_s, one_r, two_s, two_r,
):
    rows = k_hbm.shape[0]
    span = rows // 2
    heads = k_hbm.shape[1] // DH
    shared = q_hbm.shape[1] // (DH * heads)
    own = w_out.shape[0]
    octet = NZL * NC * own
    piece = NC * own
    scale = 1.0 / DH**0.5

    dp, ctx = lax.axis_index("dp"), lax.axis_index("ctx")
    cycle = NX * NZL * NC
    zhi, y = dp // NY, dp % NY
    x, zlo, core = ctx // (NZL * NC), (ctx // NC) % NZL, ctx % NC
    z = zhi * NZL + zlo
    after, before = (ctx + 1) % cycle, (ctx + cycle - 1) % cycle

    def device(x, y, z, e):
        return ((z // NZL) * NY + y, x * (NZL * NC) + (z % NZL) * NC + (core + e) % NC)

    def in_x(d, e):
        return device((x + d) % NX, y, z, e)

    def in_y(d, e):
        return device(x, (y + d) % NY, z, e)

    def in_z(d, e):
        return device(x, y, (z + d) % NZ, e)

    rings = ((y, in_y), (z, in_z))

    def spot(kind, d):
        return (rings[kind][0] + d) % NZ

    def remote(src, dst, send, recv, to):
        copy = pltpu.make_async_remote_copy(
            src_ref=src, dst_ref=dst, send_sem=send, recv_sem=recv, device_id=to, device_id_type=MESH
        )
        copy.start()

    def wait(array, sem):
        pltpu.make_async_copy(array, array, sem).wait()

    partners = [(dp, after), (dp, before)]
    partners += [in_x(d, e) for d in range(NX) for e in range(NC) if d or e]
    partners += [where(d, e) for _, where in rings for d in range(1, NZ) for e in range(NC)]
    barrier = pltpu.get_barrier_semaphore()
    load_x = pltpu.make_async_copy(x_hbm, x_v, loc.at[0])
    load_x.start()
    for to in partners:
        pl.semaphore_signal(barrier, inc=1, device_id=to, device_id_type=MESH)

    here = pl.ds(rows, rows)
    load_order = pltpu.make_async_copy(order_hbm, order, loc.at[1])
    load_lens = pltpu.make_async_copy(lens_hbm, lens, loc.at[2])
    load_order.start()
    load_lens.start()
    for i, array in enumerate((k_hbm, v_hbm)):
        pltpu.make_async_copy(array, kv_v.at[i, here], loc.at[3]).start()
    for i, array in enumerate((q_hbm, og_hbm)):
        pltpu.make_async_copy(array, qo_v.at[i], loc.at[4]).start()

    load_x.wait()
    two = 2 * NX * octet
    with jax.named_scope("turn"):
        for i in range(NZH * NY // 2):
            turned = jnp.transpose(x_v[:, i * two : (i + 1) * two])
            xt[2 * i : 2 * i + 2] = turned.reshape(2, NX, octet, rows)

    with jax.named_scope("barrier_wait"):
        pl.semaphore_wait(barrier, len(partners))

    there = pl.ds(0, rows)

    def head_cols(c):
        return pl.ds(c * DH, DH)

    for c in range(heads):
        for i, src in enumerate((k_hbm, v_hbm)):
            remote(src.at[:, head_cols(c)], kv_v.at[i, there, head_cols(c)], kv_s.at[0], kv_r.at[c], (dp, after))

    def slots(d, count=1, e=0):
        return pl.ds((e * NX + d) * rows, count * rows)

    for d in (2, 3, 1):
        remote(xt.at[:, (x + d) % NX], xr.at[:, :, slots(d)], x_s.at[0], x_r.at[d], in_x(d, 0))
    own_x = pltpu.make_async_copy(xt.at[:, x], xr.at[:, :, slots(0)], loc.at[5])
    own_x.start()

    load_order.wait()
    load_lens.wait()
    prior = (ctx + cycle - 1) % cycle
    key_slots = [order[0, 2 * prior], order[0, 2 * prior + 1], order[0, 2 * ctx], order[0, 2 * ctx + 1]]
    bounds = [lens[0, 0]]
    for i in range(1, lens.shape[1] - 1):
        bounds.append(bounds[-1] + lens[0, i])

    def rank(pos):
        seg = jnp.zeros(pos.shape, jnp.int32)
        for bound in bounds:
            seg = seg + (pos >= bound).astype(jnp.int32)
        return seg

    shape = (2 * rows, rows)
    key_at = lax.broadcasted_iota(jnp.int32, shape, 0)
    query_at = lax.broadcasted_iota(jnp.int32, shape, 1)
    key_slot = jnp.where(
        key_at < rows,
        jnp.where(key_at < span, key_slots[0], key_slots[1]),
        jnp.where(key_at < rows + span, key_slots[2], key_slots[3]),
    )
    query_slot = jnp.where(query_at < span, key_slots[2], key_slots[3])
    key_pos = key_slot * span + key_at % span
    query_pos = query_slot * span + query_at % span
    allowed = (key_pos <= query_pos) & (rank(key_pos) == rank(query_pos))
    term = jnp.where(allowed, 0.0, -1e30).astype(F32)
    bias[...] = term

    own_x.wait()

    def hand(d):
        remote(xr.at[:, :, slots(d)], xr.at[:, :, slots(d, 1, 1)], hand_s.at[0], hand_r.at[0], in_x(0, 1))

    hand(0)
    wait(kv_v.at[:, here], loc.at[3])
    wait(qo_v, loc.at[4])

    def attend(c):
        keys, values = kv_v[0, :, head_cols(c)], kv_v[1, :, head_cols(c)]
        cols = [head_cols(c * shared + j) for j in range(shared)]
        query = jnp.concatenate([qo_v[0, :, col] for col in cols], axis=0)
        grad = jnp.concatenate([qo_v[1, :, col] for col in cols], axis=0)
        score = dot(keys, query, NT) + jnp.concatenate([bias[...]] * shared, axis=1)
        dprob = dot(values, grad, NT)
        top = jnp.max(score, axis=0, keepdims=True)
        expo = jnp.exp2((score - top) * (scale * math.log2(math.e)))
        prob = expo * (1.0 / jnp.sum(expo, axis=0, keepdims=True))
        prob_low = prob.astype(BF16)
        delta = jnp.sum(prob_low.astype(F32) * dprob, axis=0, keepdims=True)
        dscore = (prob * (dprob - delta)).astype(BF16)
        key_sum = dot(dscore, query, NN) * scale
        value_sum = dot(prob_low, grad, NN)
        back[c, 0] = key_sum[:rows].astype(BF16)
        back[c, 1] = value_sum[:rows].astype(BF16)
        remote(back.at[c], brecv.at[c], b_s.at[0], b_r.at[c], (dp, before))
        acc[c, 0] = key_sum[rows:]
        acc[c, 1] = value_sum[rows:]
        query_grad = (dot(dscore, keys, TN) * scale).astype(BF16)
        for j, col in enumerate(cols):
            qg_v[:, col] = query_grad[j * rows : (j + 1) * rows]

    for c in range(heads):
        with jax.named_scope("kv_wait"):
            wait(kv_v.at[:, there, head_cols(c)], kv_r.at[c])
        with jax.named_scope(f"attention{c}"):
            attend(c)
        cols = pl.ds(c * shared * DH, shared * DH)
        pltpu.make_async_copy(qg_v.at[:, cols], qg_out.at[:, cols], out_sem.at[0]).start()

    def finish(c):
        with jax.named_scope("back_wait"):
            wait(brecv.at[c], b_r.at[c])
        for t in range(2):
            kvg[c, t] = (acc[c, t] + brecv[c, t].astype(F32)).astype(BF16)
        for d, e in ((2, 0), (2, 1), (1, 0), (3, 0), (1, 1), (3, 1), (0, 1)):
            if d != 2 or c not in RELAYED:
                remote(kvg.at[c, (core + e) % NC], gbuf.at[c, e * NX + d], g_s.at[0], g_r.at[c, int(d == 2)], in_x(d, e))
        gbuf[c, 0] = kvg[c, core]
        for t in range(2):
            pltpu.make_async_copy(kvg.at[c, t], kv_out.at[:, head_cols(t * heads + c)], out_sem.at[1]).start()

    with jax.named_scope("kv_grad0"):
        finish(0)
    with jax.named_scope("kv_grad1"):
        finish(1)
    with jax.named_scope("x_wait3"):
        wait(xr.at[:, :, slots(3)], x_r.at[3])
    hand(3)
    with jax.named_scope("kv_grad2"):
        finish(2)
    with jax.named_scope("kv_grad3"):
        finish(3)
    with jax.named_scope("x_wait1"):
        wait(xr.at[:, :, slots(1)], x_r.at[1])
    hand(1)
    with jax.named_scope("x_wait2"):
        wait(xr.at[:, :, slots(2)], x_r.at[2])
    hand(2)

    def send_first(c, kind):
        for d in FAR:
            remote(
                sent.at[c, kind, spot(kind, d)], got.at[c, kind, d - 1], one_s.at[0], one_r.at[c, kind],
                rings[kind][1](d, 0),
            )

    def join(one, other):
        lane = lax.broadcasted_iota(jnp.int32, one.shape, 1)
        return jnp.where(lane < DH // 2, one, other)

    def swap(value):
        return pltpu.roll(value, DH // 2, 1)

    def multiply(c):
        with jax.named_scope("g_wait"):
            if c not in RELAYED:
                wait(gbuf.at[c, pl.ds(0, NX * NC - 3)], g_r.at[c, 0])
            wait(gbuf.at[c, pl.ds(0, NC)], g_r.at[c, 1])
        parts = [
            dot(
                xr[h * NY : (h + 1) * NY].reshape(NY * octet, NX * NC * rows),
                gbuf[c].reshape(NX * NC * rows, DH), NN,
            )
            for h in range(NZH)
        ]
        sent[c, 0] = join(parts[0], swap(parts[1])).astype(BF16).reshape(NY, octet, DH)
        send_first(c, 0)
        middle = NY * octet // 2
        for h in range(NZH):
            pf[h] = join(swap(parts[h][:middle]), parts[h][middle:])
            for i in range(NY // 2):
                for j in range(NZL):
                    zf[h * NZL + j, i * piece : (i + 1) * piece] = pf[
                        h, i * octet + j * piece : i * octet + (j + 1) * piece
                    ]
        sent[c, 1] = zf[...].astype(BF16)
        send_first(c, 1)

    def reduce(c, kind):
        with jax.named_scope("last_wait"):
            wait(got.at[c, kind], one_r.at[c, kind])
        total = sent[c, kind, spot(kind, 0)].astype(F32)
        for i in range(NY - 1):
            total = total + got[c, kind, i].astype(F32)
        tt[c, kind, :octet] = total

    def second(q, kind):
        one, other = tt[2 * q, kind], tt[2 * q + 1, kind]
        mm[0] = join(one, swap(other))
        mm[1] = join(swap(one), other)
        for h in range(2):
            for k in range(NZL * NC):
                s2[q, kind, h * NZL + k // NC, k % NC] = mm[h, k * own : k * own + PAD].astype(BF16)
        for d in FAR + (0,):
            for e in range(NC):
                if d or e:
                    remote(
                        s2.at[q, kind, spot(1 - kind, d), (core + e) % NC], r2.at[q, kind, d * NC + e],
                        two_s.at[0], two_r.at[q, kind], rings[1 - kind][1](d, e),
                    )
        r2[q, kind, 0] = s2[q, kind, spot(1 - kind, 0), core]

    def total_of(q, kind):
        with jax.named_scope("second_wait"):
            wait(r2.at[q, kind, pl.ds(1, NY * NC - 1)], two_r.at[q, kind])
        sums = []
        for e in range(NC):
            total = r2[q, kind, e].astype(F32)
            for d in range(1, NY):
                total = total + r2[q, kind, d * NC + e].astype(F32)
            sums.append(total)
        return sums

    tt[:, :, octet:] = jnp.zeros((heads, 2, tt.shape[2] - octet, DH), F32)
    with jax.named_scope("hand_wait"):
        wait(xr.at[:, :, slots(0, NX, 1)], hand_r.at[0])

    def both(stage, c):
        with jax.named_scope(f"{stage.__name__}{c}"):
            stage(c, 0)
            stage(c, 1)

    with jax.named_scope("product0"):
        multiply(0)
    with jax.named_scope("product1"):
        multiply(1)
    with jax.named_scope("product2"):
        multiply(2)
    with jax.named_scope("product3"):
        multiply(3)
    both(reduce, 0)
    both(reduce, 1)
    both(second, 0)
    both(reduce, 2)
    both(reduce, 3)
    both(second, 1)

    with jax.named_scope("sends"):
        wait(kv_v.at[:, there], kv_s.at[0])
        wait(xr.at[:, :, slots(1, NX - 1)], x_s.at[0])
        wait(xr.at[:, :, slots(0, NX, 1)], hand_s.at[0])
        wait(brecv, b_s.at[0])
        wait(gbuf.at[:, pl.ds(1, NX * NC - 1)], g_s.at[0])
        wait(got, one_s.at[0])
        pltpu.make_async_copy(qg_v, qg_out, out_sem.at[0]).wait()
        wait(kv_out, out_sem.at[1])

    for q in range(heads // 2):
        one, other = total_of(q, 0), total_of(q, 1)
        for e in range(NC):
            for i, value in enumerate((join(one[e], swap(other[e])), join(swap(one[e]), other[e]))):
                col = (((core + e) % NC) * heads + 2 * q + i) * DH
                wv[:, pl.ds(pl.multiple_of(col, DH), DH)] = value[:own]
    with jax.named_scope("last"):
        copy = pltpu.make_async_copy(wv, w_out, out_sem.at[2])
        copy.start()
        wait(r2.at[:, :, pl.ds(1, NY * NC - 1)], two_s.at[0])
        copy.wait()


def place(qg_in, kv_in, w_in, qg_out, kv_out, w_out, qg, kv, w, got, put):
    rows = qg.shape[0] // 4
    plan = [(qg_in, qg_out, qg, pl.ds(i * rows, rows)) for i in range(4)]
    plan += [(kv_in, kv_out, kv, pl.ds(i * 2 * rows, 2 * rows)) for i in range(2)]
    plan += [(w_in, w_out, w, pl.ds(0, w.shape[0]))]
    loads = [pltpu.make_async_copy(a.at[r], v.at[r], got.at[i]) for i, (a, _, v, r) in enumerate(plan)]
    stores = [pltpu.make_async_copy(v.at[r], b.at[r], put.at[i]) for i, (_, b, v, r) in enumerate(plan)]
    for load in loads:
        load.start()
    for load, store in zip(loads, stores):
        load.wait()
        store.start()
    for store in stores:
        store.wait()


def body(queries, keys, values, out_grad, inputs, permutation, lengths):
    rows, model = inputs.shape
    heads = keys.shape[1] // DH
    own = model // (NZH * NY * NX * NZL * NC)
    octet = NZL * NC * own
    room = -(-(octet - own + PAD) // 8) * 8
    vmem = lambda kind, *shape: pltpu.VMEM(shape, kind)
    dma = lambda *shape: pltpu.SemaphoreType.DMA(shape)
    scratch = [
        pltpu.SMEM(permutation.shape, jnp.int32),
        pltpu.SMEM(lengths.shape, jnp.int32),
        vmem(BF16, rows, model),
        vmem(BF16, 2, *queries.shape),
        vmem(BF16, 2, 2 * rows, heads * DH),
        vmem(F32, 2 * rows, rows),
        vmem(BF16, *queries.shape),
        vmem(F32, heads, 2, rows, DH),
        vmem(BF16, heads, 2, rows, DH),
        vmem(BF16, heads, 2, rows, DH),
        vmem(BF16, heads, 2, rows, DH),
        vmem(BF16, heads, NX * NC, rows, DH),
        vmem(BF16, NZH * NY, NX, octet, rows),
        vmem(BF16, NZH * NY, octet, NX * NC * rows),
        vmem(F32, NZH, NY * octet // 2, DH),
        vmem(F32, NZ, octet, DH),
        vmem(BF16, heads, 2, NY, octet, DH),
        vmem(BF16, heads, 2, NY - 1, octet, DH),
        vmem(F32, heads, 2, room, DH),
        vmem(F32, 2, room, DH),
        vmem(BF16, heads // 2, 2, NY, NC, PAD, DH),
        vmem(BF16, heads // 2, 2, NY * NC, PAD, DH),
        vmem(F32, own, 2 * heads * DH),
        dma(6), dma(3),
        dma(1), dma(heads),
        dma(1), dma(NX), dma(1), dma(1),
        dma(1), dma(heads),
        dma(1), dma(heads, 2),
        dma(1), dma(heads, 2),
        dma(1), dma(heads // 2, 2),
    ]
    anywhere = pl.BlockSpec(memory_space=pl.ANY)
    shapes = (
        jax.ShapeDtypeStruct(queries.shape, BF16),
        jax.ShapeDtypeStruct((rows, 2 * heads * DH), BF16),
        jax.ShapeDtypeStruct((own, 2 * heads * DH), F32),
    )
    results = pl.pallas_call(
        kernel,
        out_shape=shapes,
        in_specs=[anywhere] * 7,
        out_specs=(anywhere,) * 3,
        scratch_shapes=scratch,
        compiler_params=pltpu.CompilerParams(
            collective_id=0, has_side_effects=True, vmem_limit_bytes=63 * 1024 * 1024
        ),
    )(permutation, lengths, queries, keys, values, out_grad, inputs)
    return pl.pallas_call(
        place,
        out_shape=shapes,
        in_specs=[anywhere] * 3,
        out_specs=(anywhere,) * 3,
        scratch_shapes=[vmem(r.dtype, *r.shape) for r in shapes] + [dma(7), dma(7)],
        compiler_params=pltpu.CompilerParams(vmem_limit_bytes=63 * 1024 * 1024),
    )(*results)


def solution(mesh):
    both = P(("dp", "ctx"), None)
    return jax.shard_map(
        body,
        mesh=mesh,
        in_specs=(both, both, both, both, both, P("dp", None), P("dp", None)),
        out_specs=(both, both, both),
        check_vma=False,
    )
```

time: 383 us -> 63.7 us (0.17); the launches traced: 378 us -> 63.6 us
  waiting for transfers between devices: 251 us -> 0 us
  Pallas kernels: 0 us -> 62.9 us
  blocking collectives: 54.2 us -> 0 us
  starting transfers between devices: 20.3 us -> 0 us
  local copies, waits for them, and re-layouts: 17.5 us -> 0 us
  between operations: 14.3 us -> 0.64 us
  matrix products: 13.1 us -> 0 us
  other arithmetic: 7.44 us -> 0 us
    reduce_scatter x1 -> x0, waiting for transfers between devices: 214 us -> none  [body(): lax.psum_scatter(term.reshape(groups, piece_width, columns), 'dp', scatte...]
    pallas_call x0 -> x2, Pallas kernels: none -> 62.9 us  [the longest x1 60.8 us: body(): pl.pallas_call(kernel, out_shape=shapes, in_specs=[anywhere] * 7, out_spe...]
    all_to_all x1 -> x0, blocking collectives: 54.2 us -> none  [body(): lax.all_to_all(spread, 'ctx', split_axis=1, concat_axis=3, tiled=True)]
    all_gather x1 -> x0, waiting for transfers between devices: 34.1 us -> none  [body(): term = folder(features, lax.all_gather(kv_grad, 'ctx', axis=0, tiled=True))]
    ppermute x4 -> x0, starting transfers between devices: 20.2 us -> none  [from_behind(): lax.ppermute(value, axis, [(i, (i + by) % size) for i in range(size)])]
    dot_general x6 -> x0, matrix products: 9.48 us -> none  [the longest x1 5.99 us: folder(): jnp.einsum('dt,tc->dc', features, piece, preferred_element_type=jnp.float32)]
    reshape x4 -> x0, local copies, waits for them, and re-layouts: 8.55 us -> none  [the longest x2 4.72 us: body(): spread = turned.reshape(groups, cycle, piece_width, rows)]
    unnamed x17 -> x0, local copies, waits for them, and re-layouts: 5.25 us -> none
  transfers between devices with their start and end apart: 6 -> 0, of which waited for: 3 -> 0; matrix products, arithmetic and copies ran while one was open for 6% -> 0% of each run, Pallas kernels for 0% -> 0%
where the time goes in v2:
time: 63.7 us; the launch traced here: 63.6 us
  Pallas kernels  62.9 us (99%)
  between operations  0.64 us (1%)
    pallas_call x1, Pallas kernels, body(): pl.pallas_call(kernel, out_shape=shapes, in_specs=[anywhere] * 7, out_spe...  60.8 us
    pallas_call x1, Pallas kernels, body(): pl.pallas_call(place, out_shape=shapes, in_specs=[anywhere] * 3, out_spec...  2.13 us

profile of v2, /device:TPU:1, one launch (start us, length us, event | category | flops | bytes accessed | tf_op | source)
XLA Modules:
  0.0 63.6 jit_solution(13622190108386106607)
XLA Ops:
  0.6 60.8 %shard_map.94 = (bf16[128,4096]{1,0:T(8,128)(2,1)}, bf16[128,1024]{1,0:T(8,128)(2,1)}, f32[10,1024]{1,0:T(8,128)}) custom-call(s32[1,64]{1,0:T(1,128)} %order_hbm.1, s32[1,4]{1,0:T(1,128)} %lens_hbm.1, bf16[128,4096]{1,0:T(8,128)(2,1)} %q_hbm.1, bf16[128,512]{1,0:T(8,128)(2,1)} %k_hbm.1, bf16[128,512]{1,0:T(8,128)(2,1)} %v_hbm.1, bf16[128,4096]{1,0:T(8,128)(2,1)} %og_hbm.1, ...), custom_call_target="tpu_custom_call" | custom-call | tf_op jit(solution)/shard_map/pallas_call | solution.py:405
  61.4 2.1 %shard_map.95 = (bf16[128,4096]{1,0:T(8,128)(2,1)}, bf16[128,1024]{1,0:T(8,128)(2,1)}, f32[10,1024]{1,0:T(8,128)}) custom-call(bf16[128,4096]{1,0:T(8,128)(2,1)} %get-tuple-element.6.qg_in, bf16[128,1024]{1,0:T(8,128)(2,1)} %get-tuple-element.7.kv_in, f32[10,1024]{1,0:T(8,128)} %get-tuple-element.8.w_in), custom_call_target="tpu_custom_call" | custom-call | tf_op jit(solution)/shard_map/pallas_call | solution.py:415

commit v3 on v2

--- a/solution.py
+++ b/solution.py
@@ -14,6 +14,8 @@
 PAD = 16
 FAR = (4, 3, 5, 2, 6, 1, 7)
 RELAYED = ()
+CUT = 48
+STEPS = (0, 1, 2)
 MESH = pl.DeviceIdType.MESH
 F32, BF16 = jnp.float32, jnp.bfloat16
 NT = (((1,), (1,)), ((), ()))
@@ -28,7 +30,7 @@
 def kernel(
     order_hbm, lens_hbm, q_hbm, k_hbm, v_hbm, og_hbm, x_hbm, qg_out, kv_out, w_out,
     order, lens, x_v, qo_v, kv_v, bias, qg_v, acc, back, brecv, kvg, gbuf, xt, xr,
-    pf, zf, sent, got, tt, mm, s2, r2, wv,
+    pf, zf, sent, comb, got, tt, mm, s2, r2, wv,
     loc, out_sem, kv_s, kv_r, x_s, x_r, hand_s, hand_r, b_s, b_r, g_s, g_r, one_s, one_r, two_s, two_r,
 ):
     rows = k_hbm.shape[0]
@@ -42,27 +44,27 @@
 
     dp, ctx = lax.axis_index("dp"), lax.axis_index("ctx")
     cycle = NX * NZL * NC
-    zhi, y = dp // NY, dp % NY
-    x, zlo, core = ctx // (NZL * NC), (ctx // NC) % NZL, ctx % NC
+    zhi, y = lax.div(dp, NY), lax.rem(dp, NY)
+    x, zlo, core = lax.div(ctx, NZL * NC), lax.rem(lax.div(ctx, NC), NZL), lax.rem(ctx, NC)
     z = zhi * NZL + zlo
-    after, before = (ctx + 1) % cycle, (ctx + cycle - 1) % cycle
+    after, before = lax.rem(ctx + 1, cycle), lax.rem(ctx + cycle - 1, cycle)
 
     def device(x, y, z, e):
-        return ((z // NZL) * NY + y, x * (NZL * NC) + (z % NZL) * NC + (core + e) % NC)
+        return (lax.div(z, NZL) * NY + y, x * (NZL * NC) + lax.rem(z, NZL) * NC + (lax.rem(core + e, NC) if e else core))
 
     def in_x(d, e):
-        return device((x + d) % NX, y, z, e)
+        return device(lax.rem(x + d, NX), y, z, e)
 
     def in_y(d, e):
-        return device(x, (y + d) % NY, z, e)
+        return device(x, lax.rem(y + NY + d, NY), z, e)
 
     def in_z(d, e):
-        return device(x, y, (z + d) % NZ, e)
+        return device(x, y, lax.rem(z + NZ + d, NZ), e)
 
     rings = ((y, in_y), (z, in_z))
 
     def spot(kind, d):
-        return (rings[kind][0] + d) % NZ
+        return lax.rem(rings[kind][0] + NZ + d, NZ)
 
     def remote(src, dst, send, recv, to):
         copy = pltpu.make_async_remote_copy(
@@ -74,8 +76,8 @@
         pltpu.make_async_copy(array, array, sem).wait()
 
     partners = [(dp, after), (dp, before)]
+    partners += [where(d, e) for d in FAR for _, where in rings for e in range(NC)]
     partners += [in_x(d, e) for d in range(NX) for e in range(NC) if d or e]
-    partners += [where(d, e) for _, where in rings for d in range(1, NZ) for e in range(NC)]
     barrier = pltpu.get_barrier_semaphore()
     load_x = pltpu.make_async_copy(x_hbm, x_v, loc.at[0])
     load_x.start()
@@ -115,13 +117,13 @@
         return pl.ds((e * NX + d) * rows, count * rows)
 
     for d in (2, 3, 1):
-        remote(xt.at[:, (x + d) % NX], xr.at[:, :, slots(d)], x_s.at[0], x_r.at[d], in_x(d, 0))
+        remote(xt.at[:, lax.rem(x + d, NX)], xr.at[:, :, slots(d)], x_s.at[0], x_r.at[d], in_x(d, 0))
     own_x = pltpu.make_async_copy(xt.at[:, x], xr.at[:, :, slots(0)], loc.at[5])
     own_x.start()
 
     load_order.wait()
     load_lens.wait()
-    prior = (ctx + cycle - 1) % cycle
+    prior = before
     key_slots = [order[0, 2 * prior], order[0, 2 * prior + 1], order[0, 2 * ctx], order[0, 2 * ctx + 1]]
     bounds = [lens[0, 0]]
     for i in range(1, lens.shape[1] - 1):
@@ -196,7 +198,7 @@
             kvg[c, t] = (acc[c, t] + brecv[c, t].astype(F32)).astype(BF16)
         for d, e in ((2, 0), (2, 1), (1, 0), (3, 0), (1, 1), (3, 1), (0, 1)):
             if d != 2 or c not in RELAYED:
-                remote(kvg.at[c, (core + e) % NC], gbuf.at[c, e * NX + d], g_s.at[0], g_r.at[c, int(d == 2)], in_x(d, e))
+                remote(kvg.at[c, lax.rem(core + e, NC)], gbuf.at[c, e * NX + d], g_s.at[0], g_r.at[c, int(d == 2)], in_x(d, e))
         gbuf[c, 0] = kvg[c, core]
         for t in range(2):
             pltpu.make_async_copy(kvg.at[c, t], kv_out.at[:, head_cols(t * heads + c)], out_sem.at[1]).start()
@@ -219,11 +221,37 @@
         wait(xr.at[:, :, slots(2)], x_r.at[2])
     hand(2)
 
+    upper, lower = pl.ds(0, CUT), pl.ds(CUT, octet - CUT)
+
     def send_first(c, kind):
-        for d in FAR:
+        def put(d, dst, last, to=None, part=pl.ds(0, octet)):
             remote(
-                sent.at[c, kind, spot(kind, d)], got.at[c, kind, d - 1], one_s.at[0], one_r.at[c, kind],
-                rings[kind][1](d, 0),
+                sent.at[c, kind, spot(kind, d), part], got.at[c, kind, dst, part], one_s.at[0],
+                one_r.at[c, kind, last], rings[kind][1](d if to is None else to, 0),
+            )
+
+        if c in STEPS:
+            put(4, 2, 0, -2, upper)
+            put(4, 2, 0, 2, lower)
+            put(-3, 0, 0, -1)
+            put(3, 1, 0, 1)
+            put(-1, 3, 1)
+            put(1, 4, 1)
+        else:
+            for d in FAR:
+                put(d, d - 1, 1)
+
+    def combine(c, kind):
+        with jax.named_scope("first_wait"):
+            wait(got.at[c, kind, pl.ds(0, 3)], one_r.at[c, kind, 0])
+        extra = got[c, kind, 2].astype(F32)
+        row = lax.broadcasted_iota(jnp.int32, extra.shape, 0)
+        for i, to in enumerate((-2, 2)):
+            total = sent[c, kind, spot(kind, to)].astype(F32) + got[c, kind, i].astype(F32)
+            mine = row < CUT if i == 0 else row >= CUT
+            comb[c, kind, i] = (total + jnp.where(mine, extra, 0.0)).astype(BF16)
+            remote(
+                comb.at[c, kind, i], got.at[c, kind, 5 + i], one_s.at[0], one_r.at[c, kind, 1], rings[kind][1](to, 0)
             )
 
     def join(one, other):
@@ -259,10 +287,11 @@
         send_first(c, 1)
 
     def reduce(c, kind):
+        first = 3 if c in STEPS else 0
         with jax.named_scope("last_wait"):
-            wait(got.at[c, kind], one_r.at[c, kind])
+            wait(got.at[c, kind, pl.ds(first, NZ - 1 - first)], one_r.at[c, kind, 1])
         total = sent[c, kind, spot(kind, 0)].astype(F32)
-        for i in range(NY - 1):
+        for i in range(first, NZ - 1):
             total = total + got[c, kind, i].astype(F32)
         tt[c, kind, :octet] = total
 
@@ -277,7 +306,7 @@
             for e in range(NC):
                 if d or e:
                     remote(
-                        s2.at[q, kind, spot(1 - kind, d), (core + e) % NC], r2.at[q, kind, d * NC + e],
+                        s2.at[q, kind, spot(1 - kind, d), lax.rem(core + e, NC)], r2.at[q, kind, d * NC + e],
                         two_s.at[0], two_r.at[q, kind], rings[1 - kind][1](d, e),
                     )
         r2[q, kind, 0] = s2[q, kind, spot(1 - kind, 0), core]
@@ -308,8 +337,11 @@
         multiply(1)
     with jax.named_scope("product2"):
         multiply(2)
+    both(combine, 0)
+    both(combine, 1)
     with jax.named_scope("product3"):
         multiply(3)
+    both(combine, 2)
     both(reduce, 0)
     both(reduce, 1)
     both(second, 0)
@@ -331,7 +363,7 @@
         one, other = total_of(q, 0), total_of(q, 1)
         for e in range(NC):
             for i, value in enumerate((join(one[e], swap(other[e])), join(swap(one[e]), other[e]))):
-                col = (((core + e) % NC) * heads + 2 * q + i) * DH
+                col = ((lax.rem(core + e, NC)) * heads + 2 * q + i) * DH
                 wv[:, pl.ds(pl.multiple_of(col, DH), DH)] = value[:own]
     with jax.named_scope("last"):
         copy = pltpu.make_async_copy(wv, w_out, out_sem.at[2])
@@ -382,6 +414,7 @@
         vmem(F32, NZH, NY * octet // 2, DH),
         vmem(F32, NZ, octet, DH),
         vmem(BF16, heads, 2, NY, octet, DH),
+        vmem(BF16, heads, 2, 2, octet, DH),
         vmem(BF16, heads, 2, NY - 1, octet, DH),
         vmem(F32, heads, 2, room, DH),
         vmem(F32, 2, room, DH),
@@ -393,7 +426,7 @@
         dma(1), dma(NX), dma(1), dma(1),
         dma(1), dma(heads),
         dma(1), dma(heads, 2),
-        dma(1), dma(heads, 2),
+        dma(1), dma(heads, 2, 2),
         dma(1), dma(heads // 2, 2),
     ]
     anywhere = pl.BlockSpec(memory_space=pl.ANY)

time: 63.7 us -> 62.9 us (0.987)
  Pallas kernels: 62.9 us -> 62.2 us
    pallas_call x1, Pallas kernels: 60.8 us -> 60 us  [body(): pl.pallas_call(kernel, out_shape=shapes, in_specs=[anywhere] * 7, out_spe...]
where the time goes in v3:
time: 62.9 us; the launch traced here: 62.8 us
  Pallas kernels  62.2 us (99%)
  between operations  0.64 us (1%)
    pallas_call x1, Pallas kernels, body(): pl.pallas_call(kernel, out_shape=shapes, in_specs=[anywhere] * 7, out_spe...  60 us
    pallas_call x1, Pallas kernels, body(): pl.pallas_call(place, out_shape=shapes, in_specs=[anywhere] * 3, out_spec...  2.13 us

profile of v3, /device:TPU:1, one launch (start us, length us, event | category | flops | bytes accessed | tf_op | source)
XLA Modules:
  0.0 62.8 jit_solution(8603137875977665949)
XLA Ops:
  0.6 60.0 %shard_map.94 = (bf16[128,4096]{1,0:T(8,128)(2,1)}, bf16[128,1024]{1,0:T(8,128)(2,1)}, f32[10,1024]{1,0:T(8,128)}) custom-call(s32[1,64]{1,0:T(1,128)} %order_hbm.1, s32[1,4]{1,0:T(1,128)} %lens_hbm.1, bf16[128,4096]{1,0:T(8,128)(2,1)} %q_hbm.1, bf16[128,512]{1,0:T(8,128)(2,1)} %k_hbm.1, bf16[128,512]{1,0:T(8,128)(2,1)} %v_hbm.1, bf16[128,4096]{1,0:T(8,128)(2,1)} %og_hbm.1, ...), custom_call_target="tpu_custom_call" | custom-call | tf_op jit(solution)/shard_map/pallas_call | solution.py:438
  60.7 2.1 %shard_map.95 = (bf16[128,4096]{1,0:T(8,128)(2,1)}, bf16[128,1024]{1,0:T(8,128)(2,1)}, f32[10,1024]{1,0:T(8,128)}) custom-call(bf16[128,4096]{1,0:T(8,128)(2,1)} %get-tuple-element.6.qg_in, bf16[128,1024]{1,0:T(8,128)(2,1)} %get-tuple-element.7.kv_in, f32[10,1024]{1,0:T(8,128)} %get-tuple-element.8.w_in), custom_call_target="tpu_custom_call" | custom-call | tf_op jit(solution)/shard_map/pallas_call | solution.py:448

commit v4 on v3

--- a/solution.py
+++ b/solution.py
@@ -116,8 +116,14 @@
     def slots(d, count=1, e=0):
         return pl.ds((e * NX + d) * rows, count * rows)
 
-    for d in (2, 3, 1):
-        remote(xt.at[:, lax.rem(x + d, NX)], xr.at[:, :, slots(d)], x_s.at[0], x_r.at[d], in_x(d, 0))
+    def blocks(h):
+        return pl.ds(h * NY, NY)
+
+    for h in range(NZH):
+        for d in (2, 3, 1):
+            remote(
+                xt.at[blocks(h), lax.rem(x + d, NX)], xr.at[blocks(h), :, slots(d)], x_s.at[0], x_r.at[h], in_x(d, 0)
+            )
     own_x = pltpu.make_async_copy(xt.at[:, x], xr.at[:, :, slots(0)], loc.at[5])
     own_x.start()
 
@@ -152,10 +158,14 @@
 
     own_x.wait()
 
-    def hand(d):
-        remote(xr.at[:, :, slots(d)], xr.at[:, :, slots(d, 1, 1)], hand_s.at[0], hand_r.at[0], in_x(0, 1))
-
-    hand(0)
+    def hand(h, d, count):
+        remote(
+            xr.at[blocks(h), :, slots(d, count)], xr.at[blocks(h), :, slots(d, count, 1)],
+            hand_s.at[0], hand_r.at[0], in_x(0, 1),
+        )
+
+    for h in range(NZH):
+        hand(h, 0, 1)
     wait(kv_v.at[:, here], loc.at[3])
     wait(qo_v, loc.at[4])
 
@@ -207,19 +217,16 @@
         finish(0)
     with jax.named_scope("kv_grad1"):
         finish(1)
-    with jax.named_scope("x_wait3"):
-        wait(xr.at[:, :, slots(3)], x_r.at[3])
-    hand(3)
+    with jax.named_scope("x_wait0"):
+        wait(xr.at[blocks(0), :, slots(1, NX - 1)], x_r.at[0])
+    hand(0, 1, NX - 1)
     with jax.named_scope("kv_grad2"):
         finish(2)
     with jax.named_scope("kv_grad3"):
         finish(3)
     with jax.named_scope("x_wait1"):
-        wait(xr.at[:, :, slots(1)], x_r.at[1])
-    hand(1)
-    with jax.named_scope("x_wait2"):
-        wait(xr.at[:, :, slots(2)], x_r.at[2])
-    hand(2)
+        wait(xr.at[blocks(1), :, slots(1, NX - 1)], x_r.at[1])
+    hand(1, 1, NX - 1)
 
     upper, lower = pl.ds(0, CUT), pl.ds(CUT, octet - CUT)
 
@@ -423,7 +430,7 @@
         vmem(F32, own, 2 * heads * DH),
         dma(6), dma(3),
         dma(1), dma(heads),
-        dma(1), dma(NX), dma(1), dma(1),
+        dma(1), dma(NZH), dma(1), dma(1),
         dma(1), dma(heads),
         dma(1), dma(heads, 2),
         dma(1), dma(heads, 2, 2),

time: 62.9 us -> 63 us (level)
  no operation moved by 1% of the time
where the time goes in v4:
time: 63 us; the launch traced here: 62.8 us
  Pallas kernels  62.2 us (99%)
  between operations  0.64 us (1%)
    pallas_call x1, Pallas kernels, body(): pl.pallas_call(kernel, out_shape=shapes, in_specs=[anywhere] * 7, out_spe...  60.1 us
    pallas_call x1, Pallas kernels, body(): pl.pallas_call(place, out_shape=shapes, in_specs=[anywhere] * 3, out_spec...  2.13 us

profile of v4, /device:TPU:1, one launch (start us, length us, event | category | flops | bytes accessed | tf_op | source)
XLA Modules:
  0.0 62.8 jit_solution(15893305944024001074)
XLA Ops:
  0.6 60.1 %shard_map.94 = (bf16[128,4096]{1,0:T(8,128)(2,1)}, bf16[128,1024]{1,0:T(8,128)(2,1)}, f32[10,1024]{1,0:T(8,128)}) custom-call(s32[1,64]{1,0:T(1,128)} %order_hbm.1, s32[1,4]{1,0:T(1,128)} %lens_hbm.1, bf16[128,4096]{1,0:T(8,128)(2,1)} %q_hbm.1, bf16[128,512]{1,0:T(8,128)(2,1)} %k_hbm.1, bf16[128,512]{1,0:T(8,128)(2,1)} %v_hbm.1, bf16[128,4096]{1,0:T(8,128)(2,1)} %og_hbm.1, ...), custom_call_target="tpu_custom_call" | custom-call | tf_op jit(solution)/shard_map/pallas_call | solution.py:445
  60.7 2.1 %shard_map.95 = (bf16[128,4096]{1,0:T(8,128)(2,1)}, bf16[128,1024]{1,0:T(8,128)(2,1)}, f32[10,1024]{1,0:T(8,128)}) custom-call(bf16[128,4096]{1,0:T(8,128)(2,1)} %get-tuple-element.6.qg_in, bf16[128,1024]{1,0:T(8,128)(2,1)} %get-tuple-element.7.kv_in, f32[10,1024]{1,0:T(8,128)} %get-tuple-element.8.w_in), custom_call_target="tpu_custom_call" | custom-call | tf_op jit(solution)/shard_map/pallas_call | solution.py:455
